TPU v7x, 512 devices: a whole 4x4x16 slice. The times are simulated.
512 devices in a mesh: span: 32 (over z_lo, x), stream: 16 (over z_hi, y, core).
Axes of the slice: x: 4, y: 4, z: 16 (z_hi: 2, z_lo: 8; z = z_hi * 8 + z_lo), core: 2. Of those that a mesh axis runs over, the one named last changes fastest.
Arguments:
- divergence: bfloat16 [1536, 512, 256], P('span', 'stream'), may hold values from -6 to 6
- flow_basis: float32 [512, 512], P('stream'), may hold values from -1 to 2
- wall_basis: float32 [256, 256], replicated, may hold values from -1 to 2
- flow_mass: float32 [512], replicated, may hold values from 0.5 to 2
- wall_mass: float32 [256], replicated, may hold values from 0.5 to 2
- flow_eigen: float32 [512], replicated, may hold values from 0.2 to 2
- wall_eigen: float32 [256], replicated, may hold values from 0.2 to 2
Outputs:
- pressure: float32 [1536, 512, 256], P(('span', 'stream'))
All inputs are finite; a program needn't handle non-finite values.
Results may differ from a plain program's by a relative error of at most 0.0023.
Values may be sent and summed in bfloat16 or wider, within the bound.
A program may use at most 64 MiB of HBM per device.

v0:
```python
import math
import jax
import jax.numpy as jnp
from jax import lax
from jax.sharding import PartitionSpec as P


def fourier_rows(field_ids, length):
    midpoint = length // 2
    wavenum = jnp.where(field_ids <= midpoint, field_ids, field_ids - midpoint)
    planes = jnp.arange(length, dtype=jnp.int32)
    phase = wavenum[:, None] * planes[None, :] % length
    angle = phase.astype(jnp.float32) * jnp.float32(2.0 * math.pi / length)
    values = jnp.where((field_ids <= midpoint)[:, None], jnp.cos(angle), -jnp.sin(angle))
    return values.astype(jnp.bfloat16)


def wave_terms(field_ids, length):
    midpoint = length // 2
    wavenum = jnp.where(field_ids <= midpoint, field_ids, field_ids - midpoint).astype(jnp.float32)
    ratio = wavenum / jnp.float32(midpoint)
    return ratio * ratio


def local(divergence, flow_basis, wall_basis, flow_mass, wall_mass, flow_eigen, wall_eigen):
    highest = lax.Precision.HIGHEST
    span_count = lax.axis_size("span")
    flow_count = lax.axis_size("stream")
    plane_count, row_count, wall_count = divergence.shape
    field_count = plane_count * span_count
    owned_fields = plane_count // flow_count
    line_length = row_count * flow_count
    rows_order = jnp.arange(field_count, dtype=jnp.int32)
    table = fourier_rows(rows_order, field_count)
    slab_in = lax.all_to_all(divergence, "span", split_axis=1, concat_axis=0, tiled=True)
    flat = jnp.dot(table, slab_in.reshape(field_count, -1), preferred_element_type=jnp.float32)
    spectral = (flat * float(field_count) ** (-0.5)).reshape(
        field_count, slab_in.shape[1], slab_in.shape[2]
    )
    grouped = lax.all_to_all(spectral, "span", split_axis=0, concat_axis=1, tiled=True)
    lines = lax.all_to_all(grouped, "stream", split_axis=0, concat_axis=1, tiled=True)
    along_wall = jnp.dot(
        (lines * wall_mass[None, None, :]).reshape(-1, wall_count), wall_basis, precision=highest
    )
    weighted = along_wall.reshape(owned_fields, line_length, wall_count) * flow_mass[None, :, None]
    owned_ids = (
        lax.axis_index("span") * plane_count
        + lax.axis_index("stream") * owned_fields
        + jnp.arange(owned_fields, dtype=jnp.int32)
    )
    waves = wave_terms(owned_ids, field_count)
    denominator = flow_eigen[None, :, None] + wall_eigen[None, None, :] + waves[:, None, None]
    coeff = jnp.einsum(
        "xn,fxm->fnm",
        lax.all_gather(flow_basis, "stream", axis=0, tiled=True),
        weighted,
        precision=highest,
    )
    solved = coeff / denominator
    back = jnp.einsum(
        "xn,fnm->fxm",
        lax.all_gather(flow_basis, "stream", axis=0, tiled=True),
        solved,
        precision=highest,
    )
    pressure = jnp.dot(back.reshape(-1, wall_count), wall_basis.T, precision=highest)
    return pressure.reshape(owned_fields, line_length, wall_count)


def solution(mesh):
    return jax.shard_map(
        local,
        mesh=mesh,
        in_specs=(P("span", "stream", None), P("stream", None), P(), P(), P(), P(), P()),
        out_specs=P(("span", "stream"), None, None),
        check_vma=False,
    )
```

profile of v0, /device:TPU:1, one launch (start us, length us, event | category | flops | bytes accessed | tf_op | source)
XLA Modules:
  0.0 348.4 jit_solution(8871368069057873704)
XLA Ops:
  6.5 0.0 copy-start
  6.5 2.5 copy.22
  9.0 15.9 %all-to-all-start = ((bf16[48,32,256]{2,0,1:T(8,128)(2,1)}), bf16[48,32,256]{2,0,1:T(8,128)(2,1)S(1)}, u32[]{:S(2)}, u32[]{:S(2)}) async-start(bf16[48,32,256]{2,0,1:T(8,128)(2,1)} %copy.22), calls=%async_computation | async-start | bytes 1572864 | tf_op jit(solution)/shard_map/all_to_all | solution.py:35
  25.0 37.8 %all-to-all-done = bf16[48,32,256]{2,0,1:T(8,128)(2,1)S(1)} async-done(((bf16[48,32,256]{2,0,1:T(8,128)(2,1)}), bf16[48,32,256]{2,0,1:T(8,128)(2,1)S(1)}, u32[]{:S(2)}, u32[]{:S(2)}) %all-to-all-start) | async-done | bytes 786464 | tf_op jit(solution)/shard_map/all_to_all | solution.py:35
  62.8 52.7 %fusion.8 = f32[1536,1,256]{2,0,1:T(8,128)S(1)} fusion(bf16[1536,256]{1,0:T(8,128)(2,1)S(1)} %bitcast.39, s32[1536]{0:T(1024)S(1)} %add_select_fusion.1, pred[1536]{0:T(1024)(128)(4,1)S(1)} %iota_compare_fusion), kind=kOutput, calls=%fused_computation.11 | convolution fusion | flops 1236664320 | bytes 2366976 | tf_op jit(solution)/shard_map/dot_general | solution.py:36
  115.5 6.5 %copy.23 = f32[1536,1,256]{2,1,0:T(1,128)S(1)} copy(f32[1536,1,256]{2,0,1:T(8,128)S(1)} %fusion.8) | data formatting | bytes 3145728 | tf_op jit(solution)/shard_map/reshape | solution.py:37
  122.0 82.2 %all_to_all.51 = f32[1536,1,256]{2,1,0:T(1,128)S(1)} all-to-all(f32[1536,1,256]{2,1,0:T(1,128)S(1)} %copy.23), channel_id=1, replica_groups=mesh['span'=32,'stream'=16] {'span'}, dimensions={0} | all-to-all | bytes 3145728 | tf_op jit(solution)/shard_map/all_to_all | solution.py:40
  204.2 0.1 copy.30
  204.3 2.1 copy.24
  206.4 0.0 copy-start.2
  206.4 0.0 copy-start.4
  206.4 12.7 %all-to-all-start.2 = ((f32[48,32,256]{2,1,0:T(8,128)}), f32[48,32,256]{2,1,0:T(8,128)S(1)}, u32[]{:S(2)}, u32[]{:S(2)}) async-start(f32[48,32,256]{2,1,0:T(8,128)} %copy.24), calls=%async_computation.2 | async-start | bytes 3145728 | tf_op jit(solution)/shard_map/all_to_all | solution.py:41
  219.0 0.2 all-gather.2.cloned.1.call-start
  219.3 0.5 all-gather.2.cloned.1.call-update
  219.8 0.0 copy-done.2
  219.8 0.0 copy-done.4
  219.8 0.1 broadcast_add_fusion
  219.9 56.0 %all-to-all-done.2 = f32[48,32,256]{2,1,0:T(8,128)S(1)} async-done(((f32[48,32,256]{2,1,0:T(8,128)}), f32[48,32,256]{2,1,0:T(8,128)S(1)}, u32[]{:S(2)}, u32[]{:S(2)}) %all-to-all-start.2) | async-done | bytes 1572896 | tf_op jit(solution)/shard_map/all_to_all | solution.py:41
  275.9 0.0 copy-start.5
  275.9 0.2 copy.25
  276.1 0.5 copy-done.5
  276.6 0.1 bitcast_multiply_fusion
  276.8 0.0 copy-done
  276.8 0.0 copy-start.3
  276.8 1.4 fusion.21
  278.2 52.6 %all-gather.2.cloned.1.call-done = f32[512,512]{1,0:T(8,128)} async-done(((f32[32,512]{1,0:T(8,128)}), f32[512,512]{1,0:T(8,128)}) %all-gather.2.cloned.1.call-update) | async-done | bytes 1048592 | tf_op jit(solution)/shard_map/all_gather | solution.py:55
  330.8 0.0 copy-done.3
  330.8 0.0 copy-start.1
  330.8 4.1 %fusion.13 = f32[3,256,512]{2,1,0:T(8,128)S(1)} fusion(f32[3,512,256]{2,1,0:T(8,128)S(1)} %fusion.21, f32[512,512]{1,0:T(8,128)} %all-gather.2.cloned.1.call-done, f32[512]{0:T(512)S(1)} %copy-done.3), kind=kOutput, calls=%fused_computation.18 | convolution fusion | flops 2416312320 | bytes 4196352 | tf_op jit(solution)/shard_map/xn,fxm->fnm/dot_general | solution.py:53
  334.9 0.0 copy-done.1
  334.9 2.8 fusion.11
  337.7 3.9 %fusion.9 = f32[3,512,256]{2,1,0:T(8,128)} fusion(f32[3,256,512]{2,1,0:T(8,128)S(1)} %fusion.11, f32[256,256]{1,0:T(8,128)S(1)} %copy-done), kind=kOutput, calls=%fused_computation.12 | convolution fusion | flops 1207959552 | bytes 3407872 | tf_op jit(solution)/shard_map/dot_general | solution.py:66
  (3 shorter events, 0.0 us)
Async XLA Ops:
  6.5 270.2 %copy-start = (f32[256,256]{1,0:T(8,128)S(1)}, f32[256,256]{1,0:T(8,128)}, u32[]{:S(2)}) copy-start(f32[256,256]{1,0:T(8,128)} %param.9) | copy-start | bytes 786436
  9.0 53.7 %all-to-all-start = ((bf16[48,32,256]{2,0,1:T(8,128)(2,1)}), bf16[48,32,256]{2,0,1:T(8,128)(2,1)S(1)}, u32[]{:S(2)}, u32[]{:S(2)}) async-start(bf16[48,32,256]{2,0,1:T(8,128)(2,1)} %copy.22), calls=%async_computation | async-start | bytes 1572864 | tf_op jit(solution)/shard_map/all_to_all | solution.py:35
  206.4 13.4 %copy-start.2 = (f32[512]{0:T(512)S(1)}, f32[512]{0:T(512)}, u32[]{:S(2)}) copy-start(f32[512]{0:T(512)} %param.12) | copy-start | bytes 6148
  206.4 13.4 %copy-start.4 = (f32[256]{0:T(256)S(1)}, f32[256]{0:T(256)}, u32[]{:S(2)}) copy-start(f32[256]{0:T(256)} %param.13) | copy-start | bytes 3076
  206.4 69.6 %all-to-all-start.2 = ((f32[48,32,256]{2,1,0:T(8,128)}), f32[48,32,256]{2,1,0:T(8,128)S(1)}, u32[]{:S(2)}, u32[]{:S(2)}) async-start(f32[48,32,256]{2,1,0:T(8,128)} %copy.24), calls=%async_computation.2 | async-start | bytes 3145728 | tf_op jit(solution)/shard_map/all_to_all | solution.py:41
  219.0 111.8 %all-gather.2.cloned.1.call-start = ((), (), s32[]{:S(2)}) async-start(), calls=%async_computation.3 | async-start | bytes 1114112 | tf_op jit(solution)/shard_map/all_gather | solution.py:55
  275.9 0.7 copy-start.5
  276.8 54.0 %copy-start.3 = (f32[512]{0:T(512)S(1)}, f32[512]{0:T(512)}, u32[]{:S(2)}) copy-start(f32[512]{0:T(512)} %param.10) | copy-start | bytes 6148
  330.8 4.1 %copy-start.1 = (f32[512,512]{1,0:T(8,128)S(1)}, f32[512,512]{1,0:T(8,128)}, u32[]{:S(2)}) copy-start(f32[512,512]{1,0:T(8,128)} %all-gather.2.cloned.1.call-done) | copy-start | bytes 3145732
Sparse Core Ops, SparseCore 0:
  223.2 107.5 all-gather.1
where the time goes:
time: 349 us; the launch traced here: 348 us
  waiting for transfers between devices  147 us (42%)
  blocking collectives  82.2 us (24%)
  matrix products  64.8 us (19%)
  starting transfers between devices  28.8 us (8%)
  between operations  13.5 us (4%)
  local copies, waits for them, and re-layouts  11.8 us (3%)
    all_to_all x1, blocking collectives, local(): lax.all_to_all(spectral, 'span', split_axis=0, concat_axis=1, tiled=True)  82.2 us
    all_to_all x1, waiting for transfers between devices, local(): lax.all_to_all(grouped, 'stream', split_axis=0, concat_axis=1, tiled=True)  56 us
    dot_general x1, matrix products, local(): jnp.dot(table, slab_in.reshape(field_count, -1), preferred_element_type=j...  52.7 us
    all_gather x1, waiting for transfers between devices, local(): lax.all_gather(flow_basis, 'stream', axis=0, tiled=True)  52.6 us
    all_to_all x1, waiting for transfers between devices, local(): lax.all_to_all(divergence, 'span', split_axis=1, concat_axis=0, tiled=True)  37.8 us
    all_to_all x1, starting transfers between devices, local(): lax.all_to_all(divergence, 'span', split_axis=1, concat_axis=0, tiled=True)  15.9 us
    all_to_all x1, starting transfers between devices, local(): lax.all_to_all(grouped, 'stream', split_axis=0, concat_axis=1, tiled=True)  12.7 us
  transfers between devices with their start and end apart: 3, of which 3 were waited for; matrix products, arithmetic and copies ran while one was open for 1% of the time, Pallas kernels for 0%

commit v1 on v0

--- a/solution.py
+++ b/solution.py
@@ -52,7 +52,10 @@
     denominator = flow_eigen[None, :, None] + wall_eigen[None, None, :] + waves[:, None, None]
     coeff = jnp.einsum(
         "xn,fxm->fnm",
-        lax.all_gather(flow_basis, "stream", axis=0, tiled=True),
+        jnp.concatenate(
+            lax.all_to_all(jnp.stack([flow_basis] * lax.axis_size("stream")), "stream", 0, 0),
+            axis=0,
+        ),
         weighted,
         precision=highest,
     )

time: 349 us -> 421 us (1.21)
  blocking collectives: 82.2 us -> 151 us
  starting transfers between devices: 28.8 us -> 43.7 us
  waiting for transfers between devices: 147 us -> 133 us
    all_to_all x0 -> x1, blocking collectives: none -> 68.8 us  [local(): lax.all_to_all(grouped, 'stream', split_axis=0, concat_axis=1, tiled=True)]
    all_to_all x1, starting transfers between devices: 12.7 us -> 27.6 us  [local(): lax.all_to_all(jnp.stack([flow_basis] * lax.axis_size('stream')), 'stream...]
    all_to_all x1, waiting for transfers between devices: 56 us -> 41.4 us  [local(): lax.all_to_all(jnp.stack([flow_basis] * lax.axis_size('stream')), 'stream...]
where the time goes in v1:
time: 421 us; the launch traced here: 420 us
  blocking collectives  151 us (36%)
  waiting for transfers between devices  133 us (32%)
  matrix products  66.4 us (16%)
  starting transfers between devices  43.7 us (10%)
  between operations  13.6 us (3%)
  local copies, waits for them, and re-layouts  11.8 us (3%)
    all_to_all x1, blocking collectives, local(): lax.all_to_all(spectral, 'span', split_axis=0, concat_axis=1, tiled=True)  82.2 us
    all_to_all x1, blocking collectives, local(): lax.all_to_all(grouped, 'stream', split_axis=0, concat_axis=1, tiled=True)  68.8 us
    all_gather x1, waiting for transfers between devices, local(): lax.all_gather(flow_basis, 'stream', axis=0, tiled=True)  53.7 us
    dot_general x1, matrix products, local(): jnp.dot(table, slab_in.reshape(field_count, -1), preferred_element_type=j...  52.7 us
    all_to_all x1, waiting for transfers between devices, local(): lax.all_to_all(jnp.stack([flow_basis] * lax.axis_size('stream')), 'stream...  41.4 us
    all_to_all x1, waiting for transfers between devices, local(): lax.all_to_all(divergence, 'span', split_axis=1, concat_axis=0, tiled=True)  37.8 us
    all_to_all x1, starting transfers between devices, local(): lax.all_to_all(jnp.stack([flow_basis] * lax.axis_size('stream')), 'stream...  27.6 us
    all_to_all x1, starting transfers between devices, local(): lax.all_to_all(divergence, 'span', split_axis=1, concat_axis=0, tiled=True)  15.9 us
  transfers between devices with their start and end apart: 3, of which 3 were waited for; matrix products, arithmetic and copies ran while one was open for 1% of the time, Pallas kernels for 0%

profile of v1, /device:TPU:1, one launch (start us, length us, event | category | flops | bytes accessed | tf_op | source)
XLA Modules:
  0.0 420.1 jit_solution(7604329062800715749)
XLA Ops:
  6.5 0.0 copy-start
  6.5 2.5 copy.22
  9.0 15.9 %all-to-all-start = ((bf16[48,32,256]{2,0,1:T(8,128)(2,1)}), bf16[48,32,256]{2,0,1:T(8,128)(2,1)S(1)}, u32[]{:S(2)}, u32[]{:S(2)}) async-start(bf16[48,32,256]{2,0,1:T(8,128)(2,1)} %copy.22), calls=%async_computation | async-start | bytes 1572864 | tf_op jit(solution)/shard_map/all_to_all | solution.py:35
  25.0 37.8 %all-to-all-done = bf16[48,32,256]{2,0,1:T(8,128)(2,1)S(1)} async-done(((bf16[48,32,256]{2,0,1:T(8,128)(2,1)}), bf16[48,32,256]{2,0,1:T(8,128)(2,1)S(1)}, u32[]{:S(2)}, u32[]{:S(2)}) %all-to-all-start) | async-done | bytes 786464 | tf_op jit(solution)/shard_map/all_to_all | solution.py:35
  62.8 52.7 %fusion.8 = f32[1536,1,256]{2,0,1:T(8,128)S(1)} fusion(bf16[1536,256]{1,0:T(8,128)(2,1)S(1)} %bitcast.42, s32[1536]{0:T(1024)S(1)} %add_select_fusion.1, pred[1536]{0:T(1024)(128)(4,1)S(1)} %iota_compare_fusion), kind=kOutput, calls=%fused_computation.11 | convolution fusion | flops 1236664320 | bytes 2366976 | tf_op jit(solution)/shard_map/dot_general | solution.py:36
  115.5 6.5 %copy.23 = f32[1536,1,256]{2,1,0:T(1,128)S(1)} copy(f32[1536,1,256]{2,0,1:T(8,128)S(1)} %fusion.8) | data formatting | bytes 3145728 | tf_op jit(solution)/shard_map/reshape | solution.py:37
  122.0 82.2 %all_to_all.56 = f32[1536,1,256]{2,1,0:T(1,128)S(1)} all-to-all(f32[1536,1,256]{2,1,0:T(1,128)S(1)} %copy.23), channel_id=1, replica_groups=mesh['span'=32,'stream'=16] {'span'}, dimensions={0} | all-to-all | bytes 3145728 | tf_op jit(solution)/shard_map/all_to_all | solution.py:40
  204.2 0.1 copy.30
  204.3 0.9 copy.24
  205.2 0.0 copy-start.1
  205.2 68.8 %all_to_all.57 = f32[48,32,256]{2,1,0:T(8,128)S(1)} all-to-all(f32[48,32,256]{2,1,0:T(8,128)S(1)} %copy.24), channel_id=1, replica_groups=mesh['span'=32,'stream'=16] {'stream'}, dimensions={0} | all-to-all | bytes 3145728 | tf_op jit(solution)/shard_map/all_to_all | solution.py:41
  274.1 0.0 copy-done.1
  274.1 1.1 stack.2
  275.2 27.6 %all-to-all-start.3 = ((f32[16,32,512]{2,1,0:T(8,128)}), f32[16,32,512]{2,1,0:T(8,128)S(1)}, u32[]{:S(2)}, u32[]{:S(2)}) async-start(f32[16,32,512]{2,1,0:T(8,128)} %stack.2), calls=%async_computation.3 | async-start | bytes 2097152 | tf_op jit(solution)/shard_map/all_to_all | solution.py:56
  302.8 0.2 all-gather.2.cloned.1.call-start
  303.0 0.5 all-gather.2.cloned.1.call-update
  303.5 0.0 copy-done.2
  303.5 0.0 copy-done.4
  303.5 0.1 broadcast_add_fusion
  303.6 0.0 copy-start.5
  303.7 0.2 copy.25
  303.8 0.5 copy-done.5
  304.3 0.1 bitcast_multiply_fusion
  304.5 0.0 copy-done
  304.5 0.0 copy-start.3
  304.5 1.4 fusion.20
  305.9 41.4 %all-to-all-done.3 = f32[16,32,512]{2,1,0:T(8,128)S(1)} async-done(((f32[16,32,512]{2,1,0:T(8,128)}), f32[16,32,512]{2,1,0:T(8,128)S(1)}, u32[]{:S(2)}, u32[]{:S(2)}) %all-to-all-start.3) | async-done | bytes 1048608 | tf_op jit(solution)/shard_map/all_to_all | solution.py:56
  347.3 0.0 copy-done.3
  347.3 3.9 fusion.13
  351.2 53.7 %all-gather.2.cloned.1.call-done = f32[512,512]{1,0:T(8,128)} async-done(((f32[32,512]{1,0:T(8,128)}), f32[512,512]{1,0:T(8,128)}) %all-gather.2.cloned.1.call-update) | async-done | bytes 1048592 | tf_op jit(solution)/shard_map/all_gather | solution.py:65
  404.9 4.5 %fusion.11 = f32[3,256,512]{2,1,0:T(8,128)S(1)} fusion(f32[3,256,512]{2,1,0:T(8,128)} %fusion.13, f32[512,512]{1,0:T(8,128)} %all-gather.2.cloned.1.call-done, f32[3]{0:T(128)S(1)} %fusion.24, f32[512,256]{0,1:T(8,128)S(1)} %broadcast_add_fusion), kind=kOutput, calls=%fused_computation.15 | convolution fusion | flops 2416705536 | bytes 4718604 | tf_op jit(solution)/shard_map/xn,fnm->fxm/dot_general | solution.py:63
  409.4 3.9 fusion.9
  (5 shorter events, 0.0 us)
Async XLA Ops:
  6.5 297.9 %copy-start = (f32[256,256]{1,0:T(8,128)S(1)}, f32[256,256]{1,0:T(8,128)}, u32[]{:S(2)}) copy-start(f32[256,256]{1,0:T(8,128)} %param.9) | copy-start | bytes 786436
  9.0 53.7 %all-to-all-start = ((bf16[48,32,256]{2,0,1:T(8,128)(2,1)}), bf16[48,32,256]{2,0,1:T(8,128)(2,1)S(1)}, u32[]{:S(2)}, u32[]{:S(2)}) async-start(bf16[48,32,256]{2,0,1:T(8,128)(2,1)} %copy.22), calls=%async_computation | async-start | bytes 1572864 | tf_op jit(solution)/shard_map/all_to_all | solution.py:35
  205.2 68.8 %copy-start.1 = (f32[32,512]{1,0:T(8,128)S(1)}, f32[32,512]{1,0:T(8,128)}, u32[]{:S(2)}) copy-start(f32[32,512]{1,0:T(8,128)} %param.8) | copy-start | bytes 196612
  274.1 29.5 %copy-start.2 = (f32[512]{0:T(512)S(1)}, f32[512]{0:T(512)}, u32[]{:S(2)}) copy-start(f32[512]{0:T(512)} %param.12) | copy-start | bytes 6148
  274.1 29.5 %copy-start.4 = (f32[256]{0:T(256)S(1)}, f32[256]{0:T(256)}, u32[]{:S(2)}) copy-start(f32[256]{0:T(256)} %param.13) | copy-start | bytes 3076
  275.2 72.2 %all-to-all-start.3 = ((f32[16,32,512]{2,1,0:T(8,128)}), f32[16,32,512]{2,1,0:T(8,128)S(1)}, u32[]{:S(2)}, u32[]{:S(2)}) async-start(f32[16,32,512]{2,1,0:T(8,128)} %stack.2), calls=%async_computation.3 | async-start | bytes 2097152 | tf_op jit(solution)/shard_map/all_to_all | solution.py:56
  302.8 102.2 %all-gather.2.cloned.1.call-start = ((), (), s32[]{:S(2)}) async-start(), calls=%async_computation.4 | async-start | bytes 1114112 | tf_op jit(solution)/shard_map/all_gather | solution.py:65
  303.6 0.7 copy-start.5
  304.5 42.8 %copy-start.3 = (f32[512]{0:T(512)S(1)}, f32[512]{0:T(512)}, u32[]{:S(2)}) copy-start(f32[512]{0:T(512)} %param.10) | copy-start | bytes 6148
Sparse Core Ops, SparseCore 0:
  306.9 97.9 all-gather.1
